TPU v7x, 32 devices: a whole 2x2x4 slice. The times are simulated.
32 devices in a mesh: rows: 8 (over z, y), hid: 4 (over x, core).
Axes of the slice: x: 2, y: 2, z: 4, core: 2. Of those that a mesh axis runs over, the one named last changes fastest.
Arguments:
- grid_input: bfloat16 [131072, 78], P('rows'), may hold values from -6 to 6
- grid_target: bfloat16 [131072, 78], P('rows'), may hold values from -6 to 6
- live_points: int32 [8], P('rows'), may hold values from 5461 to 16384, as said below
- level_weight: int32 [78], replicated, may hold values from 1 to 10
- g2m_index: int32 [16384, 8], P('rows'), may hold values from 0 to 16383
- m2m_index: int32 [16384, 6], P('rows'), may hold values from 0 to 2047
- m2g_index: int32 [131072, 3], P('rows'), may hold values from 0 to 2047
- grid_first: float32 [78, 256], P(None, 'hid'), may hold values from -0.625 to 0.625
- wide_first: float32 [3, 512, 256], P(None, None, 'hid'), may hold values from -0.25 to 0.25
- second_layer: float32 [3, 256, 256], P(None, 'hid'), may hold values from -0.375 to 0.375
- decode_second: float32 [256, 78], P('hid'), may hold values from -0.375 to 0.375
- hidden_bias: float32 [4, 256], P(None, 'hid'), may hold values from -3 to 3
- norm_params: float32 [2, 3, 256], replicated, may hold values from 0.5 to 1.5
- decode_bias: float32 [78], replicated, may hold values from -2 to 2
- grid_first_avg: float32 [78, 256], P(None, 'hid'), may hold values from -0.0008544922 to 0.0008544922
- wide_first_avg: float32 [3, 512, 256], P(None, None, 'hid'), may hold values from -0.0008544922 to 0.0008544922
- second_layer_avg: float32 [3, 256, 256], P(None, 'hid'), may hold values from -0.0008544922 to 0.0008544922
- decode_second_avg: float32 [256, 78], P('hid'), may hold values from -0.0008544922 to 0.0008544922
- hidden_bias_avg: float32 [4, 256], P(None, 'hid'), may hold values from -0.0034179688 to 0.0034179688
- norm_params_avg: float32 [2, 3, 256], replicated, may hold values from -0.0034179688 to 0.0034179688
- decode_bias_avg: float32 [78], replicated, may hold values from -0.0034179688 to 0.0034179688
- grid_first_sq: float32 [78, 256], P(None, 'hid'), may hold values from 3.0517577e-09 to 1.2207031e-08
- wide_first_sq: float32 [3, 512, 256], P(None, None, 'hid'), may hold values from 3.0517577e-09 to 1.2207031e-08
- second_layer_sq: float32 [3, 256, 256], P(None, 'hid'), may hold values from 3.0517577e-09 to 1.2207031e-08
- decode_second_sq: float32 [256, 78], P('hid'), may hold values from 3.0517577e-09 to 1.2207031e-08
- hidden_bias_sq: float32 [4, 256], P(None, 'hid'), may hold values from 4.8828124e-08 to 1.953125e-07
- norm_params_sq: float32 [2, 3, 256], replicated, may hold values from 4.8828124e-08 to 1.953125e-07
- decode_bias_sq: float32 [78], replicated, may hold values from 4.8828124e-08 to 1.953125e-07
Outputs:
- loss_total: float32 [], replicated
- loss_weight: float32 [], replicated
- grid_first_new: float32 [78, 256], P(None, 'hid')
- wide_first_new: float32 [3, 512, 256], P(None, None, 'hid')
- second_layer_new: float32 [3, 256, 256], P(None, 'hid')
- decode_second_new: float32 [256, 78], P('hid')
- hidden_bias_new: float32 [4, 256], P(None, 'hid')
- norm_params_new: float32 [2, 3, 256], replicated
- decode_bias_new: float32 [78], replicated
- grid_first_avg_new: float32 [78, 256], P(None, 'hid')
- wide_first_avg_new: float32 [3, 512, 256], P(None, None, 'hid')
- second_layer_avg_new: float32 [3, 256, 256], P(None, 'hid')
- decode_second_avg_new: float32 [256, 78], P('hid')
- hidden_bias_avg_new: float32 [4, 256], P(None, 'hid')
- norm_params_avg_new: float32 [2, 3, 256], replicated
- decode_bias_avg_new: float32 [78], replicated
- grid_first_sq_new: float32 [78, 256], P(None, 'hid')
- wide_first_sq_new: float32 [3, 512, 256], P(None, None, 'hid')
- second_layer_sq_new: float32 [3, 256, 256], P(None, 'hid')
- decode_second_sq_new: float32 [256, 78], P('hid')
- hidden_bias_sq_new: float32 [4, 256], P(None, 'hid')
- norm_params_sq_new: float32 [2, 3, 256], replicated
- decode_bias_sq_new: float32 [78], replicated
- grid_first_half: bfloat16 [78, 256], P(None, 'hid')
- wide_first_half: bfloat16 [3, 512, 256], P(None, None, 'hid')
- second_layer_half: bfloat16 [3, 256, 256], P(None, 'hid')
- decode_second_half: bfloat16 [256, 78], P('hid')
Inputs may be any that keep to these rules, and one draw needn't show every extreme that they name: `live_points`: index 0 of rows holds 5461 live points, the last index 16384; the counts never fall along rows.
All inputs are finite; a program needn't handle non-finite values.
Results may differ from a plain program's by a relative error of at most 0.00145.
The roundings to bfloat16 on the way count: a program that leaves them out, or rounds other values in their place, can miss the bound.
Values may be sent and summed in bfloat16 or wider, within the bound.
A program may use at most 320 MiB of HBM per device.

v0:
```python
import functools

import jax
import jax.numpy as jnp
from jax import lax
from jax.experimental import pallas as pl
from jax.experimental.pallas import tpu as pltpu
from jax.sharding import PartitionSpec as P

STEP_COUNT = 5
MESH = pl.DeviceIdType.MESH
bf16 = jnp.bfloat16
f32 = jnp.float32
TILE = 512
PAD = 80
COLS = {"g1": 0, "g2": 128, "e1": 384, "e2": 896, "n1": 1152, "n2": 1664, "d1": 1920, "d2": 2432}
GROUPS = {"g": (0, 384), "e": (384, 768), "n": (1152, 768), "d": (1920, 640)}
PACK = 2560


def mm(left, right):
    return lax.dot_general(left, right, (((1,), (0,)), ((), ())), preferred_element_type=f32)


def mt(left, right):
    return lax.dot_general(left, right, (((1,), (1,)), ((), ())), preferred_element_type=f32)


def flip(values):
    return values.astype(f32).T.astype(bf16)


def split2(values):
    high = values.astype(bf16)
    low = (values - high.astype(f32)).astype(bf16)
    return high, low


def fold(values):
    total = values[:, :128]
    for at in range(128, values.shape[1], 128):
        total = total + values[:, at : at + 128]
    return total


def ones_at(index, base, rows):
    lanes = index.shape[1]
    local = lax.broadcasted_iota(jnp.int32, (256, lanes), 0).astype(f32).astype(bf16)
    parts = []
    for block in range(rows // 256):
        total = None
        for k in range(index.shape[0]):
            shifted = (index[k : k + 1] - (base + block * 256)).astype(f32).astype(bf16)
            hit = jnp.where(
                jnp.broadcast_to(shifted, (256, lanes)) == local,
                jnp.asarray(1, bf16),
                jnp.asarray(0, bf16),
            )
            total = hit if total is None else total + hit
        parts.append(total)
    return parts


def act_forward(pre):
    sigma = 0.5 * jnp.tanh(0.5 * pre) + 0.5
    act = pre * sigma
    return act.astype(bf16), sigma + act * (1.0 - sigma)


def norm_forward(values):
    size = values.shape[0]
    centre = values - jnp.sum(values, 0, keepdims=True) * (1.0 / size)
    var = jnp.sum(centre * centre, 0, keepdims=True) * (1.0 / size)
    scale = lax.rsqrt(var + 1e-05)
    return centre * scale, scale


def norm_backward(upstream, normed, scale, gain):
    size = upstream.shape[0]
    scaled = upstream * gain
    first = jnp.sum(scaled, 0, keepdims=True) * (1.0 / size)
    second = jnp.sum(scaled * normed, 0, keepdims=True) * (1.0 / size)
    return scale * (scaled - first - normed * second)


class Mail:
    def __init__(self, send, recv):
        self.send, self.recv, self.used = send, recv, 0

    def copy(self, source, target, device):
        at = self.used
        self.used += 1
        if self.send is None:
            return None
        copy = pltpu.make_async_remote_copy(
            src_ref=source,
            dst_ref=target,
            send_sem=self.send.at[at],
            recv_sem=self.recv.at[at],
            device_id=device,
            device_id_type=MESH,
        )
        copy.start()
        return copy


def count_copies(row_groups):
    near = min(row_groups, 8)
    far = row_groups // near
    sums = 3 + (row_groups - 1)
    rows_sum = 3 * (2 + 2 * (near // 2 - 1)) + 2 * (near - 1) + 4 * (far - 1)
    return 15 + 9 + 6 + 2 * sums + 4 * 3 + rows_sum


def put(ref, at, values):
    for c in range(0, TILE, 128):
        ref[pl.ds(pl.multiple_of(at + 2 * c, 256), 256), :] = values[:, c : c + 128]


def take(ref, at):
    return jnp.concatenate(
        [ref[pl.ds(pl.multiple_of(at + 2 * c, 256), 256), :] for c in range(0, TILE, 128)], 1
    )


def main_kernel(
    live_ref,
    pick_ref,
    xt_hbm,
    tt_hbm,
    g2m_hbm,
    m2m_hbm,
    m2g_hbm,
    first_hbm,
    wide_hbm,
    second_hbm,
    last_hbm,
    hbias_hbm,
    norm_hbm,
    dbias_hbm,
    level_hbm,
    out_ref,
    all_ref,
    tot_ref,
    xt,
    tt,
    g2m_ref,
    m2m_ref,
    m2g_ref,
    first_f,
    last_f,
    hbias_f,
    norm_f,
    dbias_f,
    level_f,
    local_sem,
    square_tmp,
    norm_ref,
    chan_ref,
    big,
    x_ref,
    w,
    wt,
    bias,
    h0full,
    h1full,
    hgfull,
    onehot,
    spots,
    act_g,
    scale_g,
    dec_in,
    dp_d,
    ds_e,
    act_e,
    hs_e,
    nrm_e,
    scale_e,
    dsum,
    land_a,
    land_b,
    half_out,
    grad,
    gland_a,
    gland_b,
    held,
    yland,
    gland,
    rland,
    fland,
    nacc,
    cacc,
    h0_mine,
    node_in,
    mesh_tmp,
    small,
    sland_h,
    sland_r,
    narrow,
    nland_h,
    nland_r,
    send,
    recv,
    *,
    row_groups,
    g2m_deg,
    m2g_deg,
):
    hid = lax.axis_index("hid")
    row = lax.axis_index("rows")
    near = min(row_groups, 8)
    far = row_groups // near
    row_near = lax.rem(row, near)
    row_far = row // near
    core = hid + 1 - 2 * lax.rem(hid, 2)
    across = lax.rem(hid + 2, 4)
    corner = lax.rem(core + 2, 4)
    mail = Mail(send, recv)
    channels, grid_rows = xt.shape
    mine = x_ref.shape[1]
    share = h0_mine.shape[1]
    mesh_rows = h0full.shape[1]
    tiles = mine // TILE
    degree = m2m_ref.shape[0]
    latent = h0_mine.shape[0]

    def peer(device):
        return {"hid": device, "rows": row}

    def row_peer(device):
        return {"hid": hid, "rows": device}

    barrier = pltpu.get_barrier_semaphore()
    for device in (core, across, corner):
        pl.semaphore_signal(barrier, inc=1, device_id=peer(device), device_id_type=MESH)
    for step in range(1, row_groups):
        pl.semaphore_signal(
            barrier,
            inc=1,
            device_id=row_peer(lax.rem(row + step, row_groups)),
            device_id_type=MESH,
        )

    my_grid = pl.multiple_of(hid * mine, mine)
    pairs = (
        (first_hbm, first_f),
        (hbias_hbm, hbias_f),
        *((second_hbm.at[k], gland_a.at[1, :, pl.ds(256 * k, 256)]) for k in range(3)),
        *((wide_hbm.at[k], gland_a.at[0, :, pl.ds(512 * k, 512)]) for k in range(3)),
        (last_hbm, last_f),
        (xt_hbm, xt),
        (norm_hbm, norm_f),
        (dbias_hbm, dbias_f),
        (level_hbm, level_f),
        (tt_hbm.at[:, pl.ds(my_grid, mine)], tt),
        (m2m_hbm, m2m_ref),
        (m2g_hbm.at[:, pl.ds(my_grid, mine)], m2g_ref),
        (g2m_hbm, g2m_ref),
    )
    fetches = [
        pltpu.make_async_copy(source, target, local_sem.at[at])
        for at, (source, target) in enumerate(pairs)
    ]
    for fetch in fetches:
        fetch.start()

    def gather_start(view):
        near_copy = mail.copy(view(hid), view(hid), peer(core))
        far_copy = mail.copy(view(hid), view(hid), peer(across))
        return near_copy, far_copy

    def gather_pass(view, copies):
        near_copy, far_copy = copies
        far_copy.wait_recv()
        return near_copy, far_copy, mail.copy(view(across), view(across), peer(core))

    def gather_wait(copies):
        near_copy, far_copy, passed = copies
        near_copy.wait_recv()
        passed.wait_recv()
        near_copy.wait_send()
        far_copy.wait_send()
        passed.wait_send()

    def rows_of(ref, block, size, start=0, width=None):
        width = ref.shape[1] if width is None else width
        return ref.at[pl.ds(pl.multiple_of(block * size, size), size), pl.ds(start, width)]

    def lanes_of(ref, block, size):
        return ref.at[:, pl.ds(pl.multiple_of(block * size, size), size)]

    own_rows = pl.ds(pl.multiple_of(hid * 64, 64), 64)
    square_tmp[...] = jnp.zeros_like(square_tmp)
    for fetch in fetches[:5]:
        fetch.wait()
    square_tmp[0:64, 0:channels] = first_f[...]
    w[own_rows, 0:128] = square_tmp[0:64, :].astype(bf16)
    square_tmp[...] = jnp.zeros_like(square_tmp)
    square_tmp[0:4, 0:64] = hbias_f[...]
    bias[own_rows, :] = square_tmp[...].T[:64]
    for layer, name in enumerate(("g2", "e2", "n2")):
        w[own_rows, COLS[name] : COLS[name] + 256] = gland_a[1, :, 256 * layer : 256 * layer + 256].astype(bf16)
    for fetch in fetches[5:9]:
        fetch.wait()
    for layer, name in enumerate(("e1", "n1", "d1")):
        w[own_rows, COLS[name] : COLS[name] + 512] = gland_a[0, :, 512 * layer : 512 * layer + 512].astype(bf16)
    square_tmp[...] = jnp.zeros_like(square_tmp)
    square_tmp[0:64, 0:channels] = last_f[...]
    w[own_rows, COLS["d2"] : COLS["d2"] + 128] = square_tmp[0:64, :].astype(bf16)
    pl.semaphore_wait(barrier, 3 + row_groups - 1)
    flights = {}
    def weights_start(name):
        start, width = GROUPS[name]
        flights[name] = gather_start(lambda block: rows_of(w, block, 64, start, width))

    weights_start("g")
    flights["b"] = gather_start(lambda block: rows_of(bias, block, 64))

    def weights_pass(name):
        if name == "b":
            flights[name] = gather_pass(lambda block: rows_of(bias, block, 64), flights[name])
            return
        start, width = GROUPS[name]
        flights[name] = gather_pass(
            lambda block: rows_of(w, block, 64, start, width), flights[name]
        )

    for fetch in fetches[9:]:
        fetch.wait()

    def padded(values, to):
        return jnp.concatenate(
            [values.astype(f32), jnp.zeros((to - channels, values.shape[1]), f32)], 0
        )

    def turn(i, carry):
        at = pl.multiple_of(i * TILE, TILE)
        big[pl.ds(at, TILE), :] = padded(xt[:, pl.ds(at, TILE)], 128).T
        return carry

    lax.fori_loop(0, grid_rows // TILE, turn, 0)
    step_rows = 16

    def pick(k, block, unroll=True):
        for half in range(share // 256):

            def rows(i, carry):
                for u in range(step_rows):
                    at = i * step_rows + u
                    nacc[block + half, pl.ds(at, 1), :] = big[
                        pl.ds(pick_ref[k, hid * share + half * 256 + at], 1), :
                    ]
                return carry

            lax.fori_loop(0, 256 // step_rows, rows, 0, unroll=unroll)

    def picked(block):
        return jnp.concatenate(
            [nacc[block + half].T[:PAD].astype(bf16) for half in range(share // 256)], 1
        )

    pick(0, 0, unroll=False)
    square_tmp[...] = jnp.zeros_like(square_tmp)
    for layer in range(3):
        square_tmp[2 * layer : 2 * layer + 2, :] = norm_f[layer][:, :128]
    norm_ref[:128, :] = square_tmp[...].T
    for layer in range(3):
        square_tmp[2 * layer : 2 * layer + 2, :] = norm_f[layer][:, 128:]
    norm_ref[128:, :] = square_tmp[...].T
    square_tmp[...] = jnp.zeros_like(square_tmp)
    square_tmp[0:1, 0:channels] = dbias_f[...]
    square_tmp[1:2, 0:channels] = level_f[...].astype(f32)
    chan_ref[...] = square_tmp[...].T[:PAD]

    for name in "gb":
        weights_pass(name)
    for name in "end":
        weights_start(name)
    gather_wait(flights["g"])
    gather_wait(flights["b"])
    b_g, b_e, b_n, b_d = (bias[:, k : k + 1] for k in range(4))
    gains = [norm_ref[:, 2 * k : 2 * k + 1] for k in range(3)]
    shifts = [norm_ref[:, 2 * k + 1 : 2 * k + 2] for k in range(3)]
    wt[:, 0:256] = flip(w[:, COLS["g2"] : COLS["g2"] + 256])
    w1g = w[:, 0:128][:, :PAD]

    def embed(inputs):
        pre = mm(w1g, inputs) + b_g
        act, slope = act_forward(pre)
        normed, scale = norm_forward(mm(wt[:, 0:256], act))
        return act, slope, normed, scale

    mesh_tmp[0] = jnp.zeros((latent, share), f32)

    def pool(i, carry):
        for half in range(2):
            inputs = picked(2 * half)
            pick(lax.rem(2 * i + half + 1, g2m_deg), 2 - 2 * half)
            mesh_tmp[0] += embed(inputs)[2] * gains[0] + shifts[0]
        return carry

    lax.fori_loop(0, g2m_deg // 2, pool, 0)
    h0_mine[...] = mesh_tmp[0] * (1.0 / g2m_deg)
    my_mesh = pl.ds(pl.multiple_of(hid * share, share), share)
    h0_half = h0_mine[...].astype(bf16)
    h0full[:, my_mesh] = h0_half
    node_in[:latent, :] = h0_half
    h0_view = functools.partial(lanes_of, h0full, size=share)
    h0_flight = gather_start(lambda block: h0_view(block))

    lane = lax.broadcasted_iota(jnp.int32, (1, TILE), 1)
    first_row = hid * mine

    def live_mask(i):
        return (first_row + i * TILE + lane < live_ref[0]).astype(f32)

    def own(i, carry):
        here = pl.ds(pl.multiple_of(i * TILE, TILE), TILE)
        inputs = padded(
            xt[:, pl.ds(pl.multiple_of(my_grid + i * TILE, TILE), TILE)], PAD
        ).astype(bf16)
        x_ref[:, here] = inputs
        act, slope, normed, scale = embed(inputs)
        put(big, 2 * i * 2 * TILE, slope)
        act_g[:, here] = act
        put(big, (2 * i + 1) * 2 * TILE, normed)
        scale_g[:, here] = scale
        dec_in[:latent, here] = (normed * gains[0] + shifts[0]).astype(bf16)
        return carry

    def own_range(a, b):
        lax.fori_loop(a, b, own, 0)

    own_range(0, tiles // 2)
    h0_flight = gather_pass(lambda block: h0_view(block), h0_flight)
    weights_pass("e")
    weights_pass("n")
    weights_pass("d")
    own_range(tiles // 2, tiles)

    cacc[...] = jnp.zeros_like(cacc)

    def squares(i, carry):
        here = pl.ds(pl.multiple_of(i * TILE, TILE), TILE)
        delta = (padded(tt[:, here], PAD) - x_ref[:, here].astype(f32)) * live_mask(i)
        cacc[0] += fold(delta * delta)
        return carry

    lax.fori_loop(0, tiles, squares, 0)
    col = lax.broadcasted_iota(jnp.int32, (PAD, 128), 1)
    live_here = jnp.clip(live_ref[0] - first_row, 0, mine).astype(f32)
    square_tmp[...] = jnp.zeros_like(square_tmp)
    square_tmp[:PAD, :] = jnp.where(
        col == 0, jnp.sum(cacc[0], 1, keepdims=True), jnp.where(col == 1, live_here, 0.0)
    )
    small[...] = square_tmp[...].T[:8]
    sum_hid = [
        mail.copy(small, sland_h.at[slot], peer(device))
        for slot, device in enumerate((core, across, corner))
    ]

    for name in "end":
        gather_wait(flights[name])
    wt[:, 256:512] = flip(w[:, COLS["e2"] : COLS["e2"] + 256])
    wt[:, 512:768] = flip(w[:, COLS["n2"] : COLS["n2"] + 256])
    wt[:128, 768:1024] = flip(w[:, COLS["d2"] : COLS["d2"] + 128])
    gather_wait(h0_flight)

    e1 = COLS["e1"]
    mesh_tmp[0] = mm(w[:, e1 : e1 + 256], node_in[:latent, :]) + b_e
    mesh_tmp[1] = jnp.zeros((latent, share), f32)

    def edge_index(k):
        return m2m_ref[pl.ds(k, 1), my_mesh]

    def fill(index, base, rows):
        for block, part in enumerate(ones_at(index, base, rows)):
            onehot[block * 256 : block * 256 + 256, :] = part

    def edge(k, carry):
        fill(edge_index(k), 0, mesh_rows)
        sent = mm(h0full[...], onehot[...]).astype(bf16)
        hs_e[k] = sent
        pre = mesh_tmp[0] + mm(w[:, e1 + 256 : e1 + 512], sent)
        act, slope = act_forward(pre)
        act_e[k] = act
        ds_e[k] = slope
        normed, scale = norm_forward(mm(wt[:, 256:512], act))
        nrm_e[k] = normed
        scale_e[pl.ds(k, 1), :] = scale
        mesh_tmp[1] += normed * gains[1] + shifts[1]
        return carry

    lax.fori_loop(0, degree, edge, 0)

    for copy in sum_hid:
        copy.wait()
    small[...] = small[...] + sland_h[0] + sland_h[1] + sland_h[2]
    sum_rows = [
        mail.copy(small, sland_r.at[step - 1], row_peer(lax.rem(row + step, row_groups)))
        for step in range(1, row_groups)
    ]
    n1 = COLS["n1"]
    node_in[latent:, :] = mesh_tmp[1].astype(bf16)
    act_n, slope_n = act_forward(mm(w[:, n1 : n1 + 512], node_in[...]) + b_n)
    normed_n, scale_n = norm_forward(mm(wt[:, 512:768], act_n))
    h1 = h0_mine[...] + (normed_n * gains[2] + shifts[2])
    ds_e[degree] = slope_n
    act_e[degree] = act_n
    nrm_e[degree] = normed_n
    scale_e[degree : degree + 1, :] = scale_n
    h1full[:, my_mesh] = h1.astype(bf16)
    h1_view = functools.partial(lanes_of, h1full, size=share)
    h1_flight = gather_start(lambda block: h1_view(block))

    for copy in sum_rows:
        copy.wait()
    totals = small[...]
    for step in range(1, row_groups):
        totals = totals + sland_r[step - 1]
    square_tmp[...] = jnp.zeros_like(square_tmp)
    square_tmp[:8, :] = totals
    totals = square_tmp[...].T[:PAD]
    count = totals[:, 1:2]
    var = totals[:, 0:1] / count + 1e-06
    d_bias = chan_ref[:, 0:1]
    level = chan_ref[:, 1:2]
    loss_weight = count * jnp.sum(level, 0, keepdims=True)
    tot_ref[...] = jnp.broadcast_to(loss_weight[:8], (8, 128))
    weight_var = level / var
    pull = 2.0 * weight_var / loss_weight
    nacc[...] = jnp.zeros_like(nacc)
    cacc[...] = jnp.zeros_like(cacc)
    grad[...] = jnp.zeros_like(grad)
    dsum[...] = jnp.zeros_like(dsum)


    def spot(i, write):
        base = my_grid + i * TILE

        def lanes(k, carry):
            at = pl.multiple_of(k * TILE, TILE)
            for block, part in enumerate(ones_at(g2m_ref[:, pl.ds(at, TILE)], base, TILE)):
                write(block, at, part)
            return carry

        lax.fori_loop(0, mesh_rows // TILE, lanes, 0)

    def spot_store(i, carry):
        def write(block, at, part):
            spots[i, block * 256 : block * 256 + 256, pl.ds(at, TILE)] = part

        spot(i, write)
        return carry

    ready = spots.shape[0]
    lax.fori_loop(0, ready - 1, spot_store, 0)
    h1_flight = gather_pass(lambda block: h1_view(block), h1_flight)
    lax.fori_loop(ready - 1, ready, spot_store, 0)
    gather_wait(h1_flight)

    def chunk(start, width, block):
        return rows_of(grad, block, 64, start, width)

    def reduce_start(name):
        start, width = GROUPS[name]
        flight = (
            mail.copy(
                chunk(start, width, corner), gland_a.at[1, :, pl.ds(start, width)], peer(core)
            ),
            mail.copy(
                chunk(start, width, core), gland_a.at[0, :, pl.ds(start, width)], peer(core)
            ),
        )
        return flight

    def reduce_across(name, flight):
        start, width = GROUPS[name]
        cols = pl.ds(start, width)
        flight[0].wait()
        view = chunk(start, width, across)
        view[...] = view[...] + gland_a[1, :, cols]
        return flight + (mail.copy(view, gland_b.at[:, cols], peer(across)),)

    def reduce_rows(name, flight):
        start, width = GROUPS[name]
        cols = pl.ds(start, width)
        flight[1].wait()
        flight[2].wait()
        part = 64 // near
        held[:, cols] = chunk(start, width, hid)[...] + gland_a[0, :, cols] + gland_b[:, cols]
        copies = []
        for step in range(1, near):
            to = lax.rem(row_near + step, near)
            copies.append(
                mail.copy(
                    held.at[pl.ds(pl.multiple_of(to * part, part), part), cols],
                    gland.at[step - 1],
                    row_peer(row_far * near + to),
                )
            )
        return copies

    def far_sum(own_part, cols, total):
        if far > 1:
            own_part[...] = total
            more = []
            for step in range(1, far):
                to = lax.rem(row_far + step, far)
                more.append(
                    mail.copy(
                        own_part,
                        fland.at[step - 1, :, cols],
                        row_peer(to * near + row_near),
                    )
                )
            for copy in more:
                copy.wait()
            for step in range(1, far):
                total = total + fland[step - 1, :, cols]
        return total

    side = lax.rem(row_near, 2)
    level = row_near // 2
    neighbour = row_far * near + 2 * level + 1 - side

    def half_rows(which):
        return pl.ds(pl.multiple_of(which * 32, 32), 32)

    def part_rows(where):
        return pl.ds(pl.multiple_of(side * 32 + where * 8, 8), 8)

    def level_peer(where):
        return row_peer(row_far * near + 2 * where + side)

    def rows_halve(name, flight):
        start, width = GROUPS[name]
        cols = pl.ds(start, width)
        flight[1].wait()
        flight[2].wait()
        held[:, cols] = chunk(start, width, hid)[...] + gland_a[0, :, cols] + gland_b[:, cols]
        return [
            mail.copy(held.at[half_rows(1 - side), cols], yland.at[:, cols], row_peer(neighbour))
        ]

    def rows_part(name, copies):
        start, width = GROUPS[name]
        cols = pl.ds(start, width)
        copies[0].wait()
        held[half_rows(side), cols] = held[half_rows(side), cols] + yland[:, cols]
        out = []
        for step in range(1, near // 2):
            to = lax.rem(level + step, near // 2)
            out.append(
                mail.copy(
                    held.at[part_rows(to), cols], rland.at[step - 1, :, cols], level_peer(to)
                )
            )
        return out

    def rows_total(name, copies):
        start, width = GROUPS[name]
        cols = pl.ds(start, width)
        for copy in copies:
            copy.wait()
        total = held[part_rows(level), cols]
        for step in range(1, near // 2):
            total = total + rland[step - 1, :, cols]
        own_part = out_ref.at[part_rows(level), cols]
        own_part[...] = far_sum(own_part, cols, total)
        out = []
        for step in range(1, near // 2):
            to = lax.rem(level + step, near // 2)
            out.append(mail.copy(own_part, own_part, level_peer(to)))
        return out

    def rows_back(name, copies):
        start, width = GROUPS[name]
        for copy in copies:
            copy.wait()
        view = out_ref.at[half_rows(side), pl.ds(start, width)]
        return [mail.copy(view, view, row_peer(neighbour))]

    def reduce_share(name, copies):
        start, width = GROUPS[name]
        cols = pl.ds(start, width)
        part = 64 // near
        shared = pl.ds(pl.multiple_of(row_near * part, part), part)
        own_part = out_ref.at[shared, cols]
        for copy in copies:
            copy.wait()
        total = held[shared, cols]
        for step in range(1, near):
            total = total + gland[step - 1]
        own_part[...] = far_sum(own_part, cols, total)
        out = []
        for step in range(1, near):
            to = lax.rem(row_near + step, near)
            out.append(mail.copy(own_part, own_part, row_peer(row_far * near + to)))
        return out

    d1, d2 = COLS["d1"], COLS["d2"]
    def decode(i, carry):
        here = pl.ds(pl.multiple_of(i * TILE, TILE), TILE)
        fill(m2g_ref[:, here], 0, mesh_rows)
        back = mm(h1full[...], onehot[...]) * (1.0 / m2g_deg)
        dec_in[latent:, here] = back.astype(bf16)
        pre = mm(w[:, d1 : d1 + 512], dec_in[:, here]) + b_d
        act, slope = act_forward(pre)
        out = mm(wt[:128, 768:1024], act)[:PAD]
        err = x_ref[:, here].astype(f32) + out + d_bias - padded(tt[:, here], PAD)
        kept = err * live_mask(i)
        cacc[1] += fold(weight_var * kept * err)
        pred_grad = pull * kept
        cacc[0] += fold(pred_grad)
        upstream = pred_grad.astype(bf16)
        act_grad = mm(w[:, d2 : d2 + 128][:, :PAD], upstream)
        pre_grad = (act_grad * slope).astype(bf16)
        dp_d[:, here] = pre_grad
        dsum[...] += mt(onehot[...], pre_grad)
        grad[:, d2 : d2 + PAD] += mt(act, upstream)
        return carry

    lax.fori_loop(0, tiles, decode, 0)

    def spread_start(view, land):
        return (
            mail.copy(view(corner), land.at[1], peer(core)),
            mail.copy(view(core), land.at[0], peer(core)),
        )

    def spread_across(view, land, land_far, out, copies):
        copies[0].wait()
        out[...] = (view(across)[...] + land[1]).astype(bf16)
        return copies + (mail.copy(out, land_far, peer(across)),)

    def spread_end(view, land, land_far, copies):
        copies[1].wait()
        copies[2].wait()
        return view(hid)[...] + land[0] + land_far[...].astype(f32)

    def view_d(block):
        return dsum.at[pl.ds(pl.multiple_of(block * share, share), share), :]

    d_flight = spread_start(view_d, land_a.at[0])
    w1d_low = flip(w[:, d1 : d1 + 256])
    wt[:, 1024:1280] = w1d_low
    d_flight = spread_across(view_d, land_a.at[0], land_b.at[0], half_out, d_flight)

    def decode_rest(i, carry):
        here = pl.ds(pl.multiple_of(i * TILE, TILE), TILE)
        pre_grad = dp_d[:, here]
        grad[:, d1 : d1 + 512] += mt(pre_grad, dec_in[:, here])
        nacc[9] += fold(pre_grad.astype(f32))
        return carry

    lax.fori_loop(0, tiles, decode_rest, 0)
    stage = {"d": reduce_start("d")}
    wt[:, 2304:2560] = flip(w[:, d1 + 256 : d1 + 512])
    wt[:, 1280:1536] = flip(w[:, n1 : n1 + 256])
    wt[:, 1536:1792] = flip(w[:, n1 + 256 : n1 + 512])
    wt[:, 1792:2048] = flip(w[:, e1 : e1 + 256])
    wt[:, 2048:2304] = flip(w[:, e1 + 256 : e1 + 512])

    def late_store(half, carry):
        def write(block, at, part):
            lanes = pl.ds(pl.multiple_of(half * mesh_rows + at, TILE), TILE)
            dec_in[block * 256 : block * 256 + 256, lanes] = part

        spot(ready + half, write)
        return carry

    def write_last(block, at, part):
        (h0full, h1full)[block][:, pl.ds(at, TILE)] = part

    lax.fori_loop(0, 2, late_store, 0)

    def write_pieces(block, at, part):
        (hs_e, act_e)[block][at // TILE] = part

    def write_whole(block, at, part):
        onehot[pl.ds(pl.multiple_of(at + block * 256, 256), 256), :] = part

    high, low = split2(spread_end(view_d, land_a.at[0], land_b.at[0], d_flight))
    stage["d"] = reduce_across("d", stage["d"])
    h1_grad = (mt(wt[:, 2304:2560], high) + mt(wt[:, 2304:2560], low)) * (1.0 / m2g_deg)
    nacc[2] += fold(h1_grad * nrm_e[degree])
    nacc[5] += fold(h1_grad)
    up_n = norm_backward(
        h1_grad, nrm_e[degree], scale_e[degree : degree + 1, :], gains[2]
    ).astype(bf16)
    n2 = COLS["n2"]
    pre_grad_n = (mm(w[:, n2 : n2 + 256], up_n) * ds_e[degree]).astype(bf16)
    mesh_tmp[0] = h1_grad + mm(wt[:, 1280:1536], pre_grad_n)
    mesh_tmp[1] = mm(wt[:, 1536:1792], pre_grad_n)

    grad[:, n2 : n2 + 256] = mt(act_e[degree], up_n)
    grad[:, n1 : n1 + 512] = mt(pre_grad_n, node_in[...])
    nacc[8] += fold(pre_grad_n.astype(f32))
    stage["n"] = reduce_start("n")

    e2 = COLS["e2"]

    def edge_back(k, carry):
        upstream = mesh_tmp[1]
        normed = nrm_e[k]
        nacc[1] += fold(upstream * normed)
        nacc[4] += fold(upstream)
        up = norm_backward(upstream, normed, scale_e[pl.ds(k, 1), :], gains[1]).astype(bf16)
        pre_grad = (mm(w[:, e2 : e2 + 256], up) * ds_e[k]).astype(bf16)
        mesh_tmp[0] += mm(wt[:, 1792:2048], pre_grad)
        grad[:, e2 : e2 + 256] += mt(act_e[k], up)
        act_e[k] = pre_grad
        nacc[7] += fold(pre_grad.astype(f32))
        return carry

    lax.fori_loop(0, degree, edge_back, 0)
    stage["d"] = rows_halve("d", stage["d"])
    stage["n"] = reduce_across("n", stage["n"])

    def senders(block):
        total = None
        for k in range(degree):
            place = k % 4 * TILE
            for half, part in enumerate(ones_at(edge_index(k), block * share, share)):
                onehot[place + half * 256 : place + half * 256 + 256, :] = part
            term = mt(onehot[place : place + TILE, :], act_e[k])
            total = term if total is None else total + term
        view_d(block)[...] = total

    senders(corner)
    e_first = mail.copy(view_d(corner), land_a.at[1, 1], peer(core))
    senders(core)
    e_flight = (e_first, mail.copy(view_d(core), land_a.at[1, 0], peer(core)))
    senders(across)
    stage["d"] = rows_part("d", stage["d"])
    e_flight = spread_across(view_d, land_a.at[1], land_b.at[1], half_out, e_flight)
    senders(hid)

    def edge_weights(k, carry):
        grad[:, e1 : e1 + 256] += mt(act_e[k], node_in[:latent, :])
        grad[:, e1 + 256 : e1 + 512] += mt(act_e[k], hs_e[k])
        return carry

    lax.fori_loop(0, degree, edge_weights, 0)
    stage["e"] = reduce_start("e")
    stage["n"] = rows_halve("n", stage["n"])
    stage["d"] = rows_total("d", stage["d"])
    high, low = split2(spread_end(view_d, land_a.at[1], land_b.at[1], e_flight))
    h0_grad = mesh_tmp[0] + mt(wt[:, 2048:2304], high) + mt(wt[:, 2048:2304], low)
    hgfull[:, my_mesh] = (h0_grad * (1.0 / g2m_deg)).astype(bf16)
    hg_view = functools.partial(lanes_of, hgfull, size=share)
    hg_flight = gather_start(lambda block: hg_view(block))


    spot(ready + 2, write_last)
    stage["n"] = rows_part("n", stage["n"])
    stage["d"] = rows_back("d", stage["d"])
    spot(ready + 3, write_pieces)
    hg_flight = gather_pass(lambda block: hg_view(block), hg_flight)
    stage["e"] = reduce_across("e", stage["e"])
    spot(ready + 4, write_whole)
    stage["n"] = rows_total("n", stage["n"])
    gather_wait(hg_flight)

    def grid_back(i, both):
        here = pl.ds(pl.multiple_of(i * TILE, TILE), TILE)
        upstream = mm(wt[:, 1024:1280], dp_d[:, here]) + both
        normed = take(big, (2 * i + 1) * 2 * TILE)
        nacc[0] += fold(upstream * normed)
        nacc[3] += fold(upstream)
        up = norm_backward(upstream, normed, scale_g[:, here], gains[0]).astype(bf16)
        pre_grad = (mm(w[:, COLS["g2"] : COLS["g2"] + 256], up) * take(big, 2 * i * 2 * TILE)).astype(bf16)
        grad[:, COLS["g2"] : COLS["g2"] + 256] += mt(act_g[:, here], up)
        grad[:, 0:PAD] += mt(pre_grad, x_ref[:, here])
        nacc[6] += fold(pre_grad.astype(f32))

    def grid_ready(i, carry):
        grid_back(i, mt(hgfull[...], spots[i]))
        return carry

    def from_blocks(blocks):
        total = None
        for at, block in enumerate(blocks):
            term = mt(hgfull[:, at * TILE : at * TILE + TILE], block[...])
            total = term if total is None else total + term
        return total

    count_m = mesh_rows // TILE
    lax.fori_loop(0, ready, grid_ready, 0)
    stage["n"] = rows_back("n", stage["n"])
    stage["e"] = rows_halve("e", stage["e"])

    def grid_late(half, carry):
        lanes = pl.ds(pl.multiple_of(half * mesh_rows, mesh_rows), mesh_rows)
        grid_back(ready + half, mt(hgfull[...], dec_in[:, lanes]))
        return carry

    lax.fori_loop(0, 2, grid_late, 0)
    dsum[0:256, :] = mt(hgfull[...], h0full[...])
    dsum[256:512, :] = mt(hgfull[...], h1full[...])
    for half, blocks in enumerate((hs_e, act_e)):
        dsum[512 + 256 * half : 768 + 256 * half, :] = from_blocks(
            [blocks.at[k] for k in range(count_m)]
        )
    both = from_blocks([onehot.at[k * TILE : k * TILE + TILE, :] for k in range(count_m)])
    dsum[1024:1280, :] = both[:, :256]
    dsum[1280:1536, :] = both[:, 256:]

    def grid_last(k, carry):
        at = pl.multiple_of(k * TILE, TILE)
        both = jnp.concatenate([dsum[pl.ds(at, 256), :], dsum[pl.ds(at + 256, 256), :]], 1)
        grid_back(ready + 2 + k, both)
        return carry

    stage["e"] = rows_part("e", stage["e"])
    lax.fori_loop(0, 3, grid_last, 0)

    block = grad[:, 0:128]
    at_col = lax.broadcasted_iota(jnp.int32, (latent, 128), 1)
    for k in range(4):
        block = jnp.where(at_col == PAD + k, jnp.sum(nacc[6 + k], 1, keepdims=True), block)
    grad[:, 0:128] = block
    stage["g"] = reduce_start("g")
    block = jnp.zeros((latent, 128), f32)
    for k in range(6):
        block = jnp.where(at_col == 2 * (k % 3) + k // 3, jnp.sum(nacc[k], 1, keepdims=True), block)
    norm_ref[...] = block
    block = norm_ref[:PAD, :]
    for k in range(2):
        block = jnp.where(col == 6 + k, jnp.sum(cacc[k], 1, keepdims=True), block)
    norm_ref[:PAD, :] = block
    narrow[...] = norm_ref[...].T[:8]
    narrow_hid = [
        mail.copy(narrow, nland_h.at[slot], peer(device))
        for slot, device in enumerate((core, across, corner))
    ]
    stage["e"] = rows_total("e", stage["e"])
    stage["g"] = reduce_across("g", stage["g"])
    for copy in narrow_hid:
        copy.wait()
    narrow[...] = narrow[...] + nland_h[0] + nland_h[1] + nland_h[2]
    narrow_rows = [
        mail.copy(narrow, nland_r.at[step - 1], row_peer(lax.rem(row + step, row_groups)))
        for step in range(1, row_groups)
    ]
    stage["e"] = rows_back("e", stage["e"])
    stage["g"] = reduce_rows("g", stage["g"])
    stage["g"] = reduce_share("g", stage["g"])
    for copy in narrow_rows:
        copy.wait()
    total = narrow[...]
    for step in range(1, row_groups):
        total = total + nland_r[step - 1]
    all_ref[...] = total
    for name in "dneg":
        for copy in stage[name]:
            copy.wait()


def adam_step(weight, avg, sq, grad, rate, decay):
    avg_new = 0.5 * avg + 0.5 * grad
    sq_new = 0.5 * sq + 0.5 * grad * grad
    fix = 1.0 - 0.5**STEP_COUNT
    step = (avg_new * (1.0 / fix)) / (jnp.sqrt(sq_new * (1.0 / fix)) + 1e-08)
    return (weight - rate * (step + decay * weight), avg_new, sq_new)


def adam_kernel(out_ref, all_ref, tot_ref, *refs):
    ins_hbm, outs_hbm, loss_ref, weight_ref = refs[:21], refs[21:46], refs[46], refs[47]
    ins, outs, turned, sem_in, sem_out = refs[48:69], refs[69:94], refs[94], refs[95], refs[96]
    fetches = [
        pltpu.make_async_copy(source, target, sem_in.at[at])
        for at, (source, target) in enumerate(zip(ins_hbm, ins))
    ]
    for fetch in fetches:
        fetch.start()
    stores = []

    def arrive(array):
        for part in (array, 7 + array, 14 + array):
            fetches[part].wait()

    def leave(array):
        for part in (array, 7 + array, 14 + array) + ((21 + array,) if array < 4 else ()):
            store = pltpu.make_async_copy(outs[part], outs_hbm[part], sem_out.at[part])
            store.start()
            stores.append(store)

    def update(array, at, grad, rate, decay):
        fresh, avg_new, sq_new = adam_step(
            ins[array][at], ins[7 + array][at], ins[14 + array][at], grad, rate, decay
        )
        outs[array][at] = fresh
        outs[7 + array][at] = avg_new
        outs[14 + array][at] = sq_new
        if array < 4:
            outs[21 + array][at] = fresh.astype(bf16)

    everything = (slice(None), slice(None))
    channels = ins[0].shape[1]
    arrive(1)
    for layer, name in enumerate(("e1", "n1", "d1")):
        update(1, (layer,) + everything, out_ref[:, COLS[name] : COLS[name] + 512], 0.05, 0.1)
    leave(1)
    arrive(2)
    for layer, name in enumerate(("g2", "e2", "n2")):
        update(2, (layer,) + everything, out_ref[:, COLS[name] : COLS[name] + 256], 0.05, 0.1)
    leave(2)
    arrive(0)
    update(0, everything, out_ref[:, 0:128][:, :channels], 0.05, 0.1)
    leave(0)
    arrive(3)
    update(3, everything, out_ref[:, COLS["d2"] : COLS["d2"] + 128][:, :channels], 0.05, 0.1)
    leave(3)
    turned[...] = out_ref[:, 0:128].T
    arrive(4)
    update(4, everything, turned[PAD : PAD + 4, :], 0.3, 0.0)
    leave(4)
    arrive(5)
    for layer in range(3):
        update(5, (layer,) + everything, all_ref[2 * layer : 2 * layer + 2, :], 0.3, 0.0)
    leave(5)
    arrive(6)
    update(6, everything, all_ref[6:7, 0:channels], 0.3, 0.0)
    leave(6)
    loss_ref[...] = jnp.sum(all_ref[7:8, 0:PAD], 1, keepdims=True)
    weight_ref[...] = tot_ref[0:1, 0:1]
    for store in stores:
        store.wait()


def body(
    grid_input,
    grid_target,
    live_points,
    level_weight,
    g2m_index,
    m2m_index,
    m2g_index,
    *params,
):
    groups = lax.axis_size("hid")
    row_groups = lax.axis_size("rows")
    masters, avgs, squares = params[:7], params[7:14], params[14:21]
    grid_rows, channels = grid_input.shape
    mesh_rows, degree = m2m_index.shape
    latent = masters[5].shape[2]
    share = mesh_rows // groups
    mine = grid_rows // groups
    g2m_deg = g2m_index.shape[1]
    m2g_deg = m2g_index.shape[1]
    whole = pl.BlockSpec(memory_space=pltpu.VMEM)
    scalar = pl.BlockSpec(memory_space=pltpu.SMEM)
    far_memory = pl.BlockSpec(memory_space=pltpu.HBM)
    g2m = g2m_index.T

    def flat(arrays):
        first, wide, second, last, bias, norm, out_bias = arrays
        return (
            first.T,
            wide.transpose(0, 2, 1),
            second,
            last,
            bias,
            norm.transpose(1, 0, 2),
            out_bias[None],
        )

    operands = flat(masters) + flat(avgs) + flat(squares)
    loads = [
        grid_input.T,
        grid_target.T,
        g2m,
        m2m_index.T,
        m2g_index.T,
        *operands[:7],
        level_weight[None],
    ]
    kept = [jax.ShapeDtypeStruct(v.shape, v.dtype) for v in loads]
    for at in (1, 4):
        kept[at] = jax.ShapeDtypeStruct((kept[at].shape[0], mine), kept[at].dtype)
    copies = count_copies(row_groups)
    near = min(row_groups, 8)
    far = row_groups // near
    summed, spare, totals = pl.pallas_call(
        functools.partial(
            main_kernel, row_groups=row_groups, g2m_deg=g2m_deg, m2g_deg=m2g_deg
        ),
        out_shape=[
            jax.ShapeDtypeStruct((64, PACK), f32),
            jax.ShapeDtypeStruct((8, 256), f32),
            jax.ShapeDtypeStruct((8, 128), f32),
        ],
        in_specs=[scalar] * 2 + [far_memory] * 13,
        out_specs=[whole] * 3,
        scratch_shapes=[pltpu.VMEM(v.shape, v.dtype) for v in kept[:6] + kept[8:]]
        + [
            pltpu.SemaphoreType.DMA((17,)),
            pltpu.VMEM((128, 128), f32),
            pltpu.VMEM((latent, 128), f32),
            pltpu.VMEM((PAD, 128), f32),
            pltpu.VMEM((grid_rows, 128), f32),
            pltpu.VMEM((PAD, mine), bf16),
            pltpu.VMEM((256, PACK), bf16),
            pltpu.VMEM((256, 2560), bf16),
            pltpu.VMEM((256, 128), f32),
            pltpu.VMEM((latent, mesh_rows), bf16),
            pltpu.VMEM((latent, mesh_rows), bf16),
            pltpu.VMEM((latent, mesh_rows), bf16),
            pltpu.VMEM((mesh_rows, TILE), bf16),
            pltpu.VMEM((3, TILE, mesh_rows), bf16),
            pltpu.VMEM((latent, mine), bf16),
            pltpu.VMEM((1, mine), f32),
            pltpu.VMEM((2 * latent, mine), bf16),
            pltpu.VMEM((latent, mine), bf16),
            pltpu.VMEM((degree + 1, latent, share), f32),
            pltpu.VMEM((degree + 1, latent, share), bf16),
            pltpu.VMEM((degree, latent, share), bf16),
            pltpu.VMEM((degree + 1, latent, share), f32),
            pltpu.VMEM((8, share), f32),
            pltpu.VMEM((mesh_rows, latent), f32),
            pltpu.VMEM((2, 2, share, latent), f32),
            pltpu.VMEM((2, share, latent), bf16),
            pltpu.VMEM((share, latent), bf16),
            pltpu.VMEM((256, PACK), f32),
            pltpu.VMEM((2, 64, PACK), f32),
            pltpu.VMEM((64, PACK), f32),
            pltpu.VMEM((64, PACK), f32),
            pltpu.VMEM((32, PACK), f32),
            pltpu.VMEM((near - 1, 64 // near, GROUPS["g"][1]), f32),
            pltpu.VMEM((near // 2 - 1, 64 // near, PACK), f32),
            pltpu.VMEM((max(far - 1, 1), 64 // near, PACK), f32),
            pltpu.VMEM((g2m_deg * share // 256, 256, 128), f32),
            pltpu.VMEM((2, PAD, 128), f32),
            pltpu.VMEM((latent, share), f32),
            pltpu.VMEM((2 * latent, share), bf16),
            pltpu.VMEM((2, latent, share), f32),
            pltpu.VMEM((8, 128), f32),
            pltpu.VMEM((3, 8, 128), f32),
            pltpu.VMEM((row_groups - 1, 8, 128), f32),
            pltpu.VMEM((8, 256), f32),
            pltpu.VMEM((3, 8, 256), f32),
            pltpu.VMEM((row_groups - 1, 8, 256), f32),
            pltpu.SemaphoreType.DMA((copies,)),
            pltpu.SemaphoreType.DMA((copies,)),
        ],
        compiler_params=pltpu.CompilerParams(
            collective_id=0, has_side_effects=True, vmem_limit_bytes=64 * 2**20
        ),
        name="step",
    )(
        live_points,
        g2m,
        *loads,
    )
    shapes = [jax.ShapeDtypeStruct(v.shape, f32) for v in operands]
    shapes += [jax.ShapeDtypeStruct(v.shape, bf16) for v in operands[:4]]
    outs = pl.pallas_call(
        adam_kernel,
        out_shape=shapes + [jax.ShapeDtypeStruct((1, 1), f32)] * 2,
        in_specs=[whole] * 3 + [far_memory] * 21,
        out_specs=[far_memory] * 25 + [whole] * 2,
        scratch_shapes=[pltpu.VMEM(v.shape, v.dtype) for v in operands + tuple(shapes)]
        + [
            pltpu.VMEM((128, 64), f32),
            pltpu.SemaphoreType.DMA((21,)),
            pltpu.SemaphoreType.DMA((25,)),
        ],
        compiler_params=pltpu.CompilerParams(vmem_limit_bytes=64 * 2**20),
        name="adam",
    )(summed, spare, totals, *operands)

    def unflat(arrays):
        first, wide, second, last, bias, norm, out_bias = arrays
        return (
            first.T,
            wide.transpose(0, 2, 1),
            second,
            last,
            bias,
            norm.transpose(1, 0, 2),
            out_bias[0],
        )

    halves = outs[21:25]
    return (
        (outs[25][0, 0], outs[26][0, 0])
        + unflat(outs[0:7])
        + unflat(outs[7:14])
        + unflat(outs[14:21])
        + (halves[0].T, halves[1].transpose(0, 2, 1), halves[2], halves[3])
    )


def solution(mesh):
    weights = (
        P(None, "hid"),
        P(None, None, "hid"),
        P(None, "hid", None),
        P("hid", None),
        P(None, "hid"),
        P(),
        P(),
    )
    in_specs = (
        P("rows", None),
        P("rows", None),
        P("rows"),
        P(),
        P("rows", None),
        P("rows", None),
        P("rows", None),
    ) + weights * 3
    out_specs = (P(), P()) + weights * 3 + weights[:4]
    return jax.shard_map(body, mesh=mesh, in_specs=in_specs, out_specs=out_specs, check_vma=False)
```

profile of v0, /device:TPU:0, one launch (start us, length us, event | category | flops | bytes accessed | tf_op | source)
XLA Modules:
  0.0 151.8 jit_solution(15468530755921977199)
XLA Ops:
  1.3 144.9 %step.1 = (f32[64,2560]{1,0:T(8,128)}, f32[8,256]{1,0:T(8,128)}, f32[8,128]{1,0:T(8,128)}) custom-call(s32[1]{0:T(128)S(6)} %copy.55.live_ref, s32[8,2048]{1,0:T(8,128)} %bitcast.40, bf16[78,16384]{1,0:T(8,128)(2,1)} %bitcast.34, bf16[78,16384]{1,0:T(8,128)(2,1)} %bitcast.35, s32[8,2048]{1,0:T(8,128)} %bitcast.41, s32[6,2048]{1,0:T(8,128)} %bitcast.45, ...), custom_call_target="tpu_custom_call" | custom-call | tf_op jit(solution)/shard_map/step/pallas_call | solution.py:1086
  146.2 5.4 %adam.1 = (f32[64,78]{1,0:T(8,128)}, f32[3,64,512]{2,1,0:T(8,128)}, f32[3,64,256]{2,1,0:T(8,128)}, f32[64,78]{1,0:T(8,128)}, f32[4,64]{1,0:T(4,128)}, /*index=5*...) custom-call(f32[64,2560]{1,0:T(8,128)} %get-tuple-element.57.out_ref, ...), custom_call_target="tpu_custom_call" | custom-call | tf_op jit(solution)/shard_map/adam/pallas_call | solution.py:1159
where the time goes:
time: 152 us
  Pallas kernels  150 us (99%)
    pallas_call x1, Pallas kernels, body(): pl.pallas_call(functools.partial(main_kernel, row_groups=row_groups, g2m_...  145 us
    pallas_call x1, Pallas kernels, body(): pl.pallas_call(adam_kernel, out_shape=shapes + [jax.ShapeDtypeStruct((1,...  5.35 us

commit v1 on v0

--- a/solution.py
+++ b/solution.py
@@ -396,11 +396,11 @@
         for half in range(2):
             inputs = picked(2 * half)
             pick(lax.rem(2 * i + half + 1, g2m_deg), 2 - 2 * half)
-            mesh_tmp[0] += embed(inputs)[2] * gains[0] + shifts[0]
+            mesh_tmp[0] += embed(inputs)[2]
         return carry
 
     lax.fori_loop(0, g2m_deg // 2, pool, 0)
-    h0_mine[...] = mesh_tmp[0] * (1.0 / g2m_deg)
+    h0_mine[...] = mesh_tmp[0] * (gains[0] * (1.0 / g2m_deg)) + shifts[0]
     my_mesh = pl.ds(pl.multiple_of(hid * share, share), share)
     h0_half = h0_mine[...].astype(bf16)
     h0full[:, my_mesh] = h0_half
@@ -431,12 +431,11 @@
     def own_range(a, b):
         lax.fori_loop(a, b, own, 0)
 
-    own_range(0, tiles // 2)
+    own_range(0, tiles)
     h0_flight = gather_pass(lambda block: h0_view(block), h0_flight)
     weights_pass("e")
     weights_pass("n")
     weights_pass("d")
-    own_range(tiles // 2, tiles)
 
     cacc[...] = jnp.zeros_like(cacc)
 
@@ -488,7 +487,7 @@
         normed, scale = norm_forward(mm(wt[:, 256:512], act))
         nrm_e[k] = normed
         scale_e[pl.ds(k, 1), :] = scale
-        mesh_tmp[1] += normed * gains[1] + shifts[1]
+        mesh_tmp[1] += normed
         return carry
 
     lax.fori_loop(0, degree, edge, 0)
@@ -501,7 +500,7 @@
         for step in range(1, row_groups)
     ]
     n1 = COLS["n1"]
-    node_in[latent:, :] = mesh_tmp[1].astype(bf16)
+    node_in[latent:, :] = (mesh_tmp[1] * gains[1] + shifts[1] * degree).astype(bf16)
     act_n, slope_n = act_forward(mm(w[:, n1 : n1 + 512], node_in[...]) + b_n)
     normed_n, scale_n = norm_forward(mm(wt[:, 512:768], act_n))
     h1 = h0_mine[...] + (normed_n * gains[2] + shifts[2])
@@ -745,8 +744,6 @@
     d_flight = spread_start(view_d, land_a.at[0])
     w1d_low = flip(w[:, d1 : d1 + 256])
     wt[:, 1024:1280] = w1d_low
-    d_flight = spread_across(view_d, land_a.at[0], land_b.at[0], half_out, d_flight)
-
     def decode_rest(i, carry):
         here = pl.ds(pl.multiple_of(i * TILE, TILE), TILE)
         pre_grad = dp_d[:, here]
@@ -754,7 +751,9 @@
         nacc[9] += fold(pre_grad.astype(f32))
         return carry
 
-    lax.fori_loop(0, tiles, decode_rest, 0)
+    lax.fori_loop(0, tiles // 2, decode_rest, 0)
+    d_flight = spread_across(view_d, land_a.at[0], land_b.at[0], half_out, d_flight)
+    lax.fori_loop(tiles // 2, tiles, decode_rest, 0)
     stage = {"d": reduce_start("d")}
     wt[:, 2304:2560] = flip(w[:, d1 + 256 : d1 + 512])
     wt[:, 1280:1536] = flip(w[:, n1 : n1 + 256])
@@ -805,7 +804,6 @@
         upstream = mesh_tmp[1]
         normed = nrm_e[k]
         nacc[1] += fold(upstream * normed)
-        nacc[4] += fold(upstream)
         up = norm_backward(upstream, normed, scale_e[pl.ds(k, 1), :], gains[1]).astype(bf16)
         pre_grad = (mm(w[:, e2 : e2 + 256], up) * ds_e[k]).astype(bf16)
         mesh_tmp[0] += mm(wt[:, 1792:2048], pre_grad)
@@ -814,9 +812,10 @@
         nacc[7] += fold(pre_grad.astype(f32))
         return carry
 
-    lax.fori_loop(0, degree, edge_back, 0)
-    stage["d"] = rows_halve("d", stage["d"])
+    nacc[4] += fold(mesh_tmp[1]) * degree
+    lax.fori_loop(0, degree // 2, edge_back, 0)
     stage["n"] = reduce_across("n", stage["n"])
+    lax.fori_loop(degree // 2, degree, edge_back, 0)
 
     def senders(block):
         total = None
@@ -828,6 +827,7 @@
             total = term if total is None else total + term
         view_d(block)[...] = total
 
+    stage["d"] = rows_halve("d", stage["d"])
     senders(corner)
     e_first = mail.copy(view_d(corner), land_a.at[1, 1], peer(core))
     senders(core)

time: 152 us -> 151 us (level)
  no operation moved by 1% of the time
where the time goes in v1:
time: 151 us
  Pallas kernels  149 us (99%)
    pallas_call x1, Pallas kernels, body(): pl.pallas_call(functools.partial(main_kernel, row_groups=row_groups, g2m_...  144 us
    pallas_call x1, Pallas kernels, body(): pl.pallas_call(adam_kernel, out_shape=shapes + [jax.ShapeDtypeStruct((1,...  5.35 us

profile of v1, /device:TPU:0, one launch (start us, length us, event | category | flops | bytes accessed | tf_op | source)
XLA Modules:
  0.0 150.6 jit_solution(9901878224326519811)
XLA Ops:
  1.3 143.7 %step.1 = (f32[64,2560]{1,0:T(8,128)}, f32[8,256]{1,0:T(8,128)}, f32[8,128]{1,0:T(8,128)}) custom-call(s32[1]{0:T(128)S(6)} %copy.55.live_ref, s32[8,2048]{1,0:T(8,128)} %bitcast.40, bf16[78,16384]{1,0:T(8,128)(2,1)} %bitcast.34, bf16[78,16384]{1,0:T(8,128)(2,1)} %bitcast.35, s32[8,2048]{1,0:T(8,128)} %bitcast.41, s32[6,2048]{1,0:T(8,128)} %bitcast.45, ...), custom_call_target="tpu_custom_call" | custom-call | tf_op jit(solution)/shard_map/step/pallas_call | solution.py:1086
  145.1 5.4 %adam.1 = (f32[64,78]{1,0:T(8,128)}, f32[3,64,512]{2,1,0:T(8,128)}, f32[3,64,256]{2,1,0:T(8,128)}, f32[64,78]{1,0:T(8,128)}, f32[4,64]{1,0:T(4,128)}, /*index=5*...) custom-call(f32[64,2560]{1,0:T(8,128)} %get-tuple-element.57.out_ref, ...), custom_call_target="tpu_custom_call" | custom-call | tf_op jit(solution)/shard_map/adam/pallas_call | solution.py:1159
